TPU v7x, 32 devices: a whole 2x2x4 slice. The times are simulated.
32 devices in a mesh: groups: 2 (over x), seq: 16 (over z, y, core).
Axes of the slice: x: 2, y: 2, z: 4, core: 2. Of those that a mesh axis runs over, the one named last changes fastest.
Arguments:
- queries: bfloat16 [12288, 4096], P(('groups', 'seq')), parts along dimension 0, may hold values from -1.796875 to 1.796875
- keys: bfloat16 [12288, 4096], P(('groups', 'seq')), parts along dimension 0, may hold values from -1.796875 to 1.796875
- values: bfloat16 [12288, 4096], P(('groups', 'seq')), parts along dimension 0, may hold values from -1.796875 to 1.796875
- out_grad: bfloat16 [12288, 4096], P(('groups', 'seq')), parts along dimension 0, may hold values from -0.59765625 to 0.59765625
- decay_rate: float32 [32, 12288], P(None, ('groups', 'seq')), parts along dimension 1, may hold values from 0 to 1
- block_parent: int32 [32], P('groups'), parts along dimension 0, may hold values from -1 to 14, as said below
- block_valid: int32 [32], P('groups'), parts along dimension 0, may hold values from 96 to 384, as said below
Outputs:
- query_grad: bfloat16 [12288, 4096], P(('groups', 'seq')), parts along dimension 0
- key_grad: bfloat16 [12288, 4096], P(('groups', 'seq')), parts along dimension 0
- value_grad: bfloat16 [12288, 4096], P(('groups', 'seq')), parts along dimension 0
There are 2 independent parts, one for each index of `groups`. A program takes and returns all parts, laid end to end along the dimension named above; each array names one. Nothing has to cross between parts.
Inputs may be any that keep to these rules, and one draw needn't show every extreme that they name: `block_parent`: blocks 0 to 3 hold the prompt in order: block c has parent c - 1, block 0 has -1. The other blocks hold 8 branches, each a run of 1 to 4 consecutive blocks, in order of their first block; a branch's first block has parent 4 - 1 and its other blocks have parent c - 1. Block 4 starts a branch, at least one branch has exactly 4 blocks and no branch has more, and the last branch has 2 or more. `block_valid`: 384 for every block except the last block of each branch.
All inputs are finite; a program needn't handle non-finite values.
Results may differ from a plain program's by a relative error of at most 0.0057.
Values sent between devices are 32-bit elements; how exact they have to be, the bound alone decides.
A program may use at most 448 MiB of HBM per device.

v0:
```python
import math

import jax
import jax.numpy as jnp
from jax import lax
from jax.sharding import PartitionSpec as P


def entering(value, axis, join, neutral, backward):
    count, mine = (lax.axis_size(axis), lax.axis_index(axis))
    pieces = jax.tree.map(lambda part: lax.all_gather(part, axis), value)
    if backward:
        pieces = jax.tree.map(lambda part: part[::-1], pieces)
        mine = count - 1 - mine
    total = jax.tree.map(
        lambda part, zero: jnp.full_like(part, 0) + jnp.asarray(zero, part.dtype), value, neutral
    )

    def hop(position, total):
        longer = join(total, jax.tree.map(lambda part: part[position], pieces))
        return jax.tree.map(lambda new, old: jnp.where(position < mine, new, old), longer, total)

    return lax.fori_loop(0, count - 1, hop, total)


def from_root(block, axis, holder):
    block = jnp.where(lax.axis_index(axis) == holder, block, jnp.zeros_like(block))
    return lax.psum(block, axis)


def cut_combine(earlier, latter):
    decay_e, load_e, flag_e = earlier
    decay_l, load_l, flag_l = latter
    restart = flag_l > 0.5
    decay_n = jnp.where(restart, decay_l, decay_e * decay_l)
    load_n = jnp.where(restart, load_l, decay_l[:, None, None] * load_e + load_l)
    return (decay_n, load_n, jnp.maximum(flag_e, flag_l))


def on_device(queries, keys, values, out_grad, decay_rate, block_parent, block_valid):
    rows = queries.shape[0]
    heads = decay_rate.shape[0]
    head_size = queries.shape[1] // heads
    block_count = lax.axis_size("seq")
    prompt_len = block_count // 4
    my_block = lax.axis_index("seq")
    positions = jnp.arange(block_count)
    start_flags = (positions >= prompt_len) & (block_parent == prompt_len - 1)
    padded_flags = jnp.concatenate([start_flags, jnp.zeros((1,), jnp.bool_)])
    own_start = padded_flags[my_block]
    next_start = padded_flags[my_block + 1]
    valid_rows = block_valid[my_block]
    live_rows = jnp.arange(rows) < valid_rows
    zero_bf = jnp.zeros((), jnp.bfloat16)
    query_m = jnp.where(live_rows[:, None], queries, zero_bf)
    key_m = jnp.where(live_rows[:, None], keys, zero_bf)
    value_m = jnp.where(live_rows[:, None], values, zero_bf)
    grad_m = jnp.where(live_rows[:, None], out_grad, zero_bf)
    log_decay = jnp.where(live_rows[None, :], -decay_rate, 0.0)
    cumulative = jnp.cumsum(log_decay, axis=1)
    tail_w = jnp.exp(cumulative[:, -1:] - cumulative)
    head_w = jnp.exp(cumulative)
    block_decay = jnp.exp(cumulative[:, -1])
    query_hd = query_m.reshape(rows, heads, head_size)
    key_hd = key_m.reshape(rows, heads, head_size)
    value_hd = value_m.reshape(rows, heads, head_size)
    grad_hd = grad_m.reshape(rows, heads, head_size)
    key_w = (tail_w.T[:, :, None] * key_hd).astype(jnp.bfloat16)
    query_w = (head_w.T[:, :, None] * query_hd).astype(jnp.bfloat16)
    local_state = jnp.einsum("shd,she->hde", key_w, value_hd, preferred_element_type=jnp.float32)
    state_grad = jnp.einsum("thd,the->hde", query_w, grad_hd, preferred_element_type=jnp.float32)
    head_group = math.gcd(heads, 8)
    group_width = head_group * head_size
    causal = jnp.arange(rows)[:, None] >= jnp.arange(rows)[None, :]

    def inner_block(turn_no, totals):
        query_sum, key_sum, value_sum = totals
        begin = turn_no * group_width
        query_grp = lax.dynamic_slice_in_dim(query_m, begin, group_width, 1).reshape(
            rows, head_group, head_size
        )
        key_grp = lax.dynamic_slice_in_dim(key_m, begin, group_width, 1).reshape(
            rows, head_group, head_size
        )
        value_grp = lax.dynamic_slice_in_dim(value_m, begin, group_width, 1).reshape(
            rows, head_group, head_size
        )
        grad_grp = lax.dynamic_slice_in_dim(grad_m, begin, group_width, 1).reshape(
            rows, head_group, head_size
        )
        cumul_grp = lax.dynamic_slice_in_dim(cumulative, turn_no * head_group, head_group, 0)
        scores = jnp.einsum("thd,shd->hts", query_grp, key_grp, preferred_element_type=jnp.float32)
        grad_dots = jnp.einsum(
            "the,she->hts", grad_grp, value_grp, preferred_element_type=jnp.float32
        )
        log_gaps = cumul_grp[:, :, None] - cumul_grp[:, None, :]
        weights = jnp.where(causal[None], jnp.exp(jnp.minimum(log_gaps, 0.0)), 0.0)
        attn_mix = (scores * weights).astype(jnp.bfloat16)
        grad_mix = (grad_dots * weights).astype(jnp.bfloat16)
        query_part = jnp.einsum(
            "hts,shd->thd", grad_mix, key_grp, preferred_element_type=jnp.float32
        ).reshape(rows, group_width)
        key_part = jnp.einsum(
            "hts,thd->shd", grad_mix, query_grp, preferred_element_type=jnp.float32
        ).reshape(rows, group_width)
        value_part = jnp.einsum(
            "hts,the->she", attn_mix, grad_grp, preferred_element_type=jnp.float32
        ).reshape(rows, group_width)
        return (
            lax.dynamic_update_slice_in_dim(query_sum, query_part, begin, 1),
            lax.dynamic_update_slice_in_dim(key_sum, key_part, begin, 1),
            lax.dynamic_update_slice_in_dim(value_sum, value_part, begin, 1),
        )

    zeros_rows = jnp.zeros((rows, heads * head_size), jnp.float32)
    query_inner, key_inner, value_inner = lax.fori_loop(
        0, heads // head_group, inner_block, (zeros_rows, zeros_rows, zeros_rows)
    )
    ones_head = jnp.ones((heads,), jnp.float32)
    zeros_state = jnp.zeros((heads, head_size, head_size), jnp.float32)
    fwd_decay = jnp.where(next_start, 1.0, block_decay)
    fwd_load = jnp.where(next_start, 0.0, local_state)
    reached = entering(
        (fwd_decay, fwd_load, next_start.astype(jnp.float32)),
        "seq",
        cut_combine,
        (ones_head, zeros_state, jnp.zeros((), jnp.float32)),
        False,
    )
    bwd_decay = jnp.where(own_start, 1.0, block_decay)
    bwd_load = jnp.where(own_start, 0.0, state_grad)
    returned = entering(
        (bwd_decay, bwd_load, own_start.astype(jnp.float32)),
        "seq",
        cut_combine,
        (ones_head, zeros_state, jnp.zeros((), jnp.float32)),
        True,
    )
    root_state = block_decay[:, None, None] * reached[1] + local_state
    start_grad = jnp.where(own_start, block_decay[:, None, None] * returned[1] + state_grad, 0.0)
    prompt_end = from_root(root_state, "seq", prompt_len - 1)
    grad_root = lax.psum(start_grad, "seq")
    state_in = reached[1] + jnp.where(
        my_block >= prompt_len, reached[0][:, None, None] * prompt_end, 0.0
    )
    grad_out = returned[1] + jnp.where(
        my_block < prompt_len, returned[0][:, None, None] * grad_root, 0.0
    )
    state_bf = state_in.astype(jnp.bfloat16)
    grad_bf = grad_out.astype(jnp.bfloat16)
    query_outer = jnp.einsum("the,hde->thd", grad_hd, state_bf, preferred_element_type=jnp.float32)
    key_outer = jnp.einsum("she,hde->shd", value_hd, grad_bf, preferred_element_type=jnp.float32)
    value_outer = jnp.einsum("shd,hde->she", key_hd, grad_bf, preferred_element_type=jnp.float32)
    query_grad = query_inner + (head_w.T[:, :, None] * query_outer).reshape(rows, heads * head_size)
    key_grad = key_inner + (tail_w.T[:, :, None] * key_outer).reshape(rows, heads * head_size)
    value_grad = value_inner + (tail_w.T[:, :, None] * value_outer).reshape(rows, heads * head_size)
    return (
        query_grad.astype(jnp.bfloat16),
        key_grad.astype(jnp.bfloat16),
        value_grad.astype(jnp.bfloat16),
    )


def solution(mesh):
    placed = (
        P(("groups", "seq"), None),
        P(("groups", "seq"), None),
        P(("groups", "seq"), None),
        P(("groups", "seq"), None),
        P(None, ("groups", "seq")),
        P("groups"),
        P("groups"),
    )
    return jax.shard_map(
        on_device,
        mesh=mesh,
        in_specs=placed,
        out_specs=(
            P(("groups", "seq"), None),
            P(("groups", "seq"), None),
            P(("groups", "seq"), None),
        ),
        check_vma=False,
    )
```

profile of v0, /device:TPU:0, one launch (start us, length us, event | category | flops | bytes accessed | tf_op | source)
XLA Modules:
  0.0 668.1 jit_solution(12135224058718062263)
XLA Ops:
  14.0 4.8 copy.54
  21.6 4.8 copy.56
  29.1 7.5 %broadcast_select_fusion.6 = (bf16[384,4096]{0,1:T(8,128)(2,1)S(1)}, bf16[384,4096]{0,1:T(8,128)(2,1)}, bf16[384,4096]{0,1:T(8,128)(2,1)}, bf16[384,4096]{0,1:T(8,128)(2,1)S(1)}) fusion(bf16[384,4096]{0,1:T(8,128)(2,1)} %copy.59, pred[384]{0:T(512)(128)(4,1)S(1)} %iota_compare_fusion.1, bf16[384,4096]{0,1:T(8,128)(2,1)} %copy.55, ...), kind=kLoop, calls=%fused_computation.45 | loop fusion | flops 6291456 | bytes 25166208 | tf_op jit(solution)/shard_map/jit(_where)/select_n | solution.py:55
  36.6 7.5 %broadcast_select_fusion.10 = (f32[32,128,128]{2,1,0:T(8,128)}, f32[32,128,128]{2,1,0:T(8,128)}) fusion(pred[]{:T(512)} %bitcast.12, bf16[384,32,128]{0,2,1:T(8,128)(2,1)} %bitcast.9, bf16[384,32,128]{0,2,1:T(8,128)(2,1)S(1)} %bitcast.132, f32[384,32]{0,1:T(8,128)S(1)} %get-tuple-element.570), kind=kOutput, calls=%fused_computation.54 | convolution fusion | flops 407896064 | bytes 10534913 | tf_op jit(solution)/shard_map/thd,the->hde/dot_general | solution.py:71
  44.3 5.9 broadcast_select_fusion.11
  54.4 36.8 %all-reduce.4 = (f32[16]{0:T(128)S(1)}, f32[512]{0:T(512)S(1)}, f32[16]{0:T(128)S(1)}, f32[512]{0:T(512)S(1)}) all-reduce(f32[16]{0:T(128)S(1)} %convert_dynamic-update-slice_fusion.1, f32[512]{0:T(512)S(1)} %dynamic-update-slice.1, f32[16]{0:T(128)S(1)} %convert_dynamic-update-slice_fusion, ...), channel_id=1, replica_groups=mesh['groups'=2,'seq'=16] {'seq'}, use_global_device_ids=true, to_apply=%add | all-reduce | flops 1056 | bytes 8448
  91.5 124.6 %all-gather.9.cloned.1.call-done = f32[512,128,128]{2,1,0:T(8,128)} async-done(((f32[32,128,128]{2,1,0:T(8,128)}), f32[512,128,128]{2,1,0:T(8,128)}) %all-gather.9.cloned.1.call-update) | async-done | bytes 33554448 | tf_op jit(solution)/shard_map/all_gather | solution.py:11
  216.1 23.4 %rev.11 = f32[16,32,128,128]{3,2,1,0:T(8,128)} reverse(f32[16,32,128,128]{3,2,1,0:T(8,128)} %bitcast.131), dimensions={0} | reverse | bytes 67108864 | tf_op jit(solution)/shard_map/rev | solution.py:13
  239.5 58.1 %while.52 = (s32[]{:T(128)}, f32[32]{0:T(128)S(1)}, f32[32,128,128]{2,1,0:T(8,128)S(1)}, s32[]{:T(128)}, f32[16]{0:T(128)S(1)}, /*index=5*/f32[16,32]{1,0:T(8,12...) while((s32[]{:T(128)}, f32[32]{0:T(128)S(1)}, ...), condition=%wide.region_8.9_spmd.clone, body=%wide.region_7.8_spmd.clone.sunk | while | flops 2621573 | bytes 6292250 | solution.py:23
  297.6 88.5 %all-gather.7.cloned.1.call-done = f32[512,128,128]{2,1,0:T(8,128)} async-done(((f32[32,128,128]{2,1,0:T(8,128)}), f32[512,128,128]{2,1,0:T(8,128)}) %all-gather.7.cloned.1.call-update) | async-done | bytes 33554448 | tf_op jit(solution)/shard_map/all_gather | solution.py:11
  386.2 77.5 %while.51 = (s32[]{:T(128)}, f32[32]{0:T(128)S(1)}, f32[32,128,128]{2,1,0:T(8,128)}, s32[]{:T(128)}, f32[16]{0:T(128)S(1)}, /*index=5*/f32[16,32]{1,0:T(8,128)S(...) while((s32[]{:T(128)}, f32[32]{0:T(128)S(1)}, f32[32,128,128]{2,1,0:T(8,128)}, ...), condition=%wide.region_5.6_spmd.clone, body=%wide.region_4.5_spmd.clone.sunk | while | flops 2621573 | bytes 6292250 | solution.py:23
  387.4 3.3 fusion.67
  392.0 3.9 fusion.67
  397.2 3.9 fusion.67
  402.4 3.9 fusion.67
  407.6 3.9 fusion.67
  412.8 3.9 fusion.67
  418.0 3.9 fusion.67
  423.3 3.9 fusion.67
  428.5 3.9 fusion.67
  433.7 3.9 fusion.67
  438.9 3.9 fusion.67
  444.1 3.9 fusion.67
  449.3 3.9 fusion.67
  454.5 3.9 fusion.67
  459.7 3.9 fusion.67
  463.6 6.8 %add_select_fusion.2 = (f32[32,128,128]{2,1,0:T(8,128)}, f32[32,128,128]{2,1,0:T(8,128)}) fusion(f32[32,128,128]{2,1,0:T(8,128)} %get-tuple-element.582, f32[32,128,128]{2,1,0:T(8,128)S(1)} %get-tuple-element.428, f32[32]{0:T(128)S(1)} %exp.37, pred[]{:T(512)} %bitcast.12, f32[32,128,128]{2,1,0:T(8,128)} %get-tuple-element.580, ...), kind=kLoop, calls=%fused_computation.50 | loop fusion | flops 3145728 | bytes 12583042 | tf_op jit(solution)/shard_map/jit(_where)/select_n | solution.py:140
  470.4 3.4 broadcast_in_dim.97.clone
  473.8 3.4 broadcast_in_dim.97.clone2
  477.2 3.5 broadcast_in_dim.97.clone2.1
  480.6 126.6 %while.50 = (s32[]{:T(128)}, f32[384,4096]{1,0:T(8,128)}, f32[384,4096]{1,0:T(8,128)}, f32[384,4096]{1,0:T(8,128)}, bf16[384,4096]{0,1:T(8,128)(2,1)}, /*index=5...) while((s32[]{:T(128)}, f32[384,4096]{1,0:T(8,128)}, ...), condition=%wide.region_3.4_spmd.clone, body=%wide.region_2.3_spmd.clone.sunk | while | flops 1521893376 | bytes 49250620 | solution.py:116
  495.3 4.7 fusion.65
  500.0 3.1 copy.102
  503.1 4.1 constant_dynamic-update-slice_fusion.6
  527.0 4.7 fusion.65
  534.8 4.0 constant_dynamic-update-slice_fusion.6
  558.7 4.7 fusion.65
  566.4 4.0 constant_dynamic-update-slice_fusion.6
  590.3 4.7 fusion.65
  598.0 4.0 constant_dynamic-update-slice_fusion.6
  609.8 5.7 bitcast_multiply_fusion.1
  615.5 3.8 bitcast_multiply_fusion
  619.2 6.5 copy.67
  625.8 6.7 %copy.71 = f32[384,4096]{1,0:T(8,128)} copy(f32[384,4096]{0,1:T(8,128)} %bitcast.135) | data formatting | bytes 12582912 | tf_op jit(solution)/shard_map/reshape | solution.py:156
  632.5 6.3 bitcast_multiply_fusion.2
  638.8 6.8 %copy.63 = f32[384,4096]{1,0:T(8,128)} copy(f32[384,4096]{0,1:T(8,128)} %bitcast.133) | data formatting | bytes 12582912 | tf_op jit(solution)/shard_map/reshape | solution.py:154
  645.6 7.3 %add_convert_fusion.2 = bf16[384,4096]{1,0:T(8,128)(2,1)} fusion(f32[384,4096]{1,0:T(8,128)} %get-tuple-element.424, f32[384,4096]{1,0:T(8,128)} %copy.63), kind=kLoop, calls=%fused_computation.39 | loop fusion | flops 3145728 | bytes 15728640 | tf_op jit(solution)/shard_map/convert_element_type | solution.py:158
  654.4 7.1 %add_convert_fusion = (bf16[384,4096]{1,0:T(8,128)(2,1)}, bf16[384,4096]{1,0:T(8,128)(2,1)}) fusion(f32[384,4096]{1,0:T(8,128)} %get-tuple-element.430, f32[384,4096]{1,0:T(8,128)S(1)} %bitcast.139, f32[384,4096]{1,0:T(8,128)} %get-tuple-element.427, f32[384,4096]{1,0:T(8,128)S(1)} %bitcast.137), kind=kLoop, calls=%fused_computation.37 | loop fusion | flops 6291456 | bytes 31457280 | tf_op jit(solution)/shard_map/convert_element_type | solution.py:160
  (208 shorter events, 167.3 us)
Async XLA Ops:
  7.2 208.9 %all-gather.9.cloned.1.call-start = ((), (), s32[]{:S(2)}) async-start(), calls=%async_computation.1 | async-start | bytes 35651584 | tf_op jit(solution)/shard_map/all_gather | solution.py:11
  14.0 4.8 copy-start.7
  21.6 4.8 copy-start.8
  36.6 7.6 %copy-start.5 = (bf16[384,4096]{0,1:T(8,128)(2,1)}, bf16[384,4096]{0,1:T(8,128)(2,1)S(1)}, u32[]{:S(2)}) copy-start(bf16[384,4096]{0,1:T(8,128)(2,1)S(1)} %get-tuple-element.746) | copy-start | bytes 9437188
  36.6 7.6 %copy-start.3 = (bf16[384,4096]{0,1:T(8,128)(2,1)}, bf16[384,4096]{0,1:T(8,128)(2,1)S(1)}, u32[]{:S(2)}) copy-start(bf16[384,4096]{0,1:T(8,128)(2,1)S(1)} %get-tuple-element.742) | copy-start | bytes 9437188
  44.2 342.0 %all-gather.7.cloned.1.call-start = ((), (), s32[]{:S(2)}) async-start(), calls=%async_computation | async-start | bytes 35651584 | tf_op jit(solution)/shard_map/all_gather | solution.py:11
  44.3 6.0 copy-start.9
  50.2 557.0 %all-reduce.8.cloned.1.call-start = ((), (), s32[]{:S(2)}) async-start(), calls=%async_computation.2 | async-start | bytes 8388608 | tf_op jit(solution)/shard_map/psum | solution.py:28
  297.6 166.0 %copy-start = (f32[32,128,128]{2,1,0:T(8,128)}, f32[32,128,128]{2,1,0:T(8,128)S(1)}, u32[]{:S(2)}) copy-start(f32[32,128,128]{2,1,0:T(8,128)S(1)} %get-tuple-element.428) | copy-start | bytes 6291460
  481.9 5.2 copy-start.6
  488.3 0.9 copy-start.2
  513.6 5.2 copy-start.6
  520.0 0.9 copy-start.2
  545.2 5.2 copy-start.6
  551.7 0.9 copy-start.2
  576.9 5.2 copy-start.6
  583.3 0.9 copy-start.2
  609.8 5.7 copy-start.4
  625.8 6.7 %copy-start.1 = (f32[32,128,128]{2,1,0:T(8,128)S(1)}, f32[32,128,128]{2,1,0:T(8,128)}, u32[]{:S(2)}) copy-start(f32[32,128,128]{2,1,0:T(8,128)} %get-tuple-element.425) | copy-start | bytes 6291460
  638.8 14.0 %slice-start.2 = ((s8[6291456]{0:T(1024)(128)(4,1)}), s8[2097152]{0:T(1024)(128)(4,1)S(1)}, s32[]{:S(2)}) async-start(s8[6291456]{0:T(1024)(128)(4,1)} %bitcast.138), calls=%async_computation.5 | async-start | bytes 4194304
  645.6 7.3 %slice-start = ((s8[6291456]{0:T(1024)(128)(4,1)}), s8[4194304]{0:T(1024)(128)(4,1)S(1)}, s32[]{:S(2)}) async-start(s8[6291456]{0:T(1024)(128)(4,1)} %bitcast.136), calls=%async_computation.3 | async-start | bytes 8388608
  645.6 7.3 %slice-start.1 = ((s8[6291456]{0:T(1024)(128)(4,1)}), s8[2097152]{0:T(1024)(128)(4,1)S(1)}, s32[]{:S(2)}) async-start(s8[6291456]{0:T(1024)(128)(4,1)} %bitcast.136), calls=%async_computation.4 | async-start | bytes 4194304
  645.6 8.8 %slice-start.3 = ((s8[6291456]{0:T(1024)(128)(4,1)}), s8[4194304]{0:T(1024)(128)(4,1)S(1)}, s32[]{:S(2)}) async-start(s8[6291456]{0:T(1024)(128)(4,1)} %bitcast.138), calls=%async_computation.6 | async-start | bytes 8388608
Sparse Core Ops, SparseCore 0:
  44.3 171.7 all-gather.8
  217.7 168.4 all-gather.6
  470.5 111.7 all-reduce.7
where the time goes:
time: 671 us; the launch traced here: 668 us
  waiting for transfers between devices  213 us (32%)
  local copies, waits for them, and re-layouts  173 us (26%)
  other arithmetic  137 us (20%)
  matrix products  74.1 us (11%)
  blocking collectives  36.8 us (5%)
  loops' own time  19.1 us (3%)
  between operations  14.5 us (2%)
    all_gather x2, waiting for transfers between devices, entering(): pieces = jax.tree.map(lambda part: lax.all_gather(part, axis), value)  213 us
    select_n x60, other arithmetic, hop(): jnp.where(position < mine, new, old)  98.7 us
    unnamed x1, blocking collectives  36.8 us
    dynamic_update_slice x8, local copies, waits for them, and re-layouts, inner_block(): lax.dynamic_update_slice_in_dim(value_sum, value_part, begin, 1)  28.3 us
    rev x3, local copies, waits for them, and re-layouts, entering(): pieces = jax.tree.map(lambda part: part[::-1], pieces)  23.5 us
    another operation x2, loops' own time, entering(): return lax.fori_loop(0, count - 1, hop, total)  18.9 us
    dot_general x4, matrix products, inner_block(): jnp.einsum('hts,the->she', attn_mix, grad_grp, preferred_element_type=jnp...  18.7 us
    dynamic_slice x30, local copies, waits for them, and re-layouts, hop(): longer = join(total, jax.tree.map(lambda part: part[position], pieces))  18 us
  transfers between devices with their start and end apart: 3, of which 2 were waited for; matrix products, arithmetic and copies ran while one was open for 32% of the time, Pallas kernels for 0%

commit v1 on v0

v1 whole, which is shorter than its diff:
```python
import functools

import jax
import jax.numpy as jnp
from jax import lax
from jax.experimental import pallas as pl
from jax.experimental.pallas import tpu as pltpu
from jax.sharding import PartitionSpec as P

F32 = jnp.float32
BF16 = jnp.bfloat16
TN = (((0,), (0,)), ((), ()))
NT = (((1,), (1,)), ((), ()))


def dot(a, b, dims=(((1,), (0,)), ((), ())), precision=None):
    return lax.dot_general(a, b, dims, precision=precision, preferred_element_type=F32)


def live_mask(valid, rows, width):
    return (lax.broadcasted_iota(jnp.int32, (rows, width), 0) < valid).astype(F32).astype(BF16)


def head_column(cum_t, head):
    lane = lax.broadcasted_iota(jnp.int32, cum_t.shape, 1)
    return jnp.sum(jnp.where(lane == head, cum_t, 0.0), axis=1, keepdims=True)


def local_kernel(per, valid, rate, q, k, v, g, state, grad, cum, cum_t, decay):
    rows = q.shape[0]
    size = state.shape[1]

    @pl.when(pl.program_id(0) == 0)
    def _():
        place = lax.broadcasted_iota(jnp.int32, rate.shape, 1)
        log_decay = jnp.where(place < valid[0], -rate[...], 0.0)
        below = lax.broadcasted_iota(jnp.int32, (rows, rows), 0) >= lax.broadcasted_iota(
            jnp.int32, (rows, rows), 1
        )
        tri = below.astype(F32)
        high = lax.Precision.HIGHEST
        cum[...] = dot(log_decay, tri, NT, high)
        cum_t[...] = dot(tri, log_decay, NT, high)
        decay[...] = jnp.broadcast_to(jnp.exp(cum[:, rows - 1 : rows]), decay.shape)

    mask = live_mask(valid[0], rows, size)
    for part in range(per):
        head = pl.program_id(0) * per + part
        cols = slice(part * size, (part + 1) * size)
        column = head_column(cum_t[...], head)
        head_w = jnp.exp(column)
        tail_w = jnp.exp(column[rows - 1 :, :] - column)
        key_w = (tail_w * (k[:, cols] * mask).astype(F32)).astype(BF16)
        query_w = (head_w * (q[:, cols] * mask).astype(F32)).astype(BF16)
        state[part] = dot(key_w, v[:, cols] * mask, TN)
        grad[part] = dot(query_w, g[:, cols] * mask, TN)


def grads_kernel(per, valid, cum, cum_t, q, k, v, g, state, grad, dq, dk, dv):
    rows = q.shape[0]
    size = state.shape[1]
    mask = live_mask(valid[0], rows, size)
    causal_t = lax.broadcasted_iota(jnp.int32, (rows, rows), 0) <= lax.broadcasted_iota(
        jnp.int32, (rows, rows), 1
    )
    for part in range(per):
        head = pl.program_id(0) * per + part
        cols = slice(part * size, (part + 1) * size)
        column = head_column(cum_t[...], head)
        row = cum[pl.ds(head, 1), :]
        head_w = jnp.exp(column)
        tail_w = jnp.exp(column[rows - 1 :, :] - column)
        qm, km, vm, gm = (ref[:, cols] * mask for ref in (q, k, v, g))
        weight_t = jnp.where(causal_t, jnp.exp(jnp.minimum(row - column, 0.0)), 0.0)
        attn_t = (dot(km, qm, NT) * weight_t).astype(BF16)
        gmix_t = (dot(vm, gm, NT) * weight_t).astype(BF16)
        dq[:, cols] = (dot(gmix_t, km, TN) + head_w * dot(gm, state[part], NT)).astype(BF16)
        dk[:, cols] = (dot(gmix_t, qm) + tail_w * dot(vm, grad[part], NT)).astype(BF16)
        dv[:, cols] = (dot(attn_t, gm) + tail_w * dot(km, grad[part])).astype(BF16)


def chain_kernel(
    n, prompt, chunk, load, gload, decay, flags, state_out, grad_out,
    r_f, r_e, r_b, r_x, r_y, s_f, s_b, s_x, send_sem, recv_sem,
):
    c = lax.axis_index("seq")
    count = load.shape[0] // chunk
    root = prompt - 1
    branch = c >= prompt
    even = lax.rem(c, 2) == 0
    node = branch & even
    inner = node & (c + 4 < n)
    partners = [
        (c > 0, c - 1),
        (c < n - 1, c + 1),
        (inner, c + 4),
        (node & (c - 4 >= prompt), c - 4),
        (c == prompt + 2, root),
        (c == root, prompt + 2),
    ]
    barrier = pltpu.get_barrier_semaphore()
    total = 0
    for cond, other in partners:
        total = total + cond.astype(jnp.int32)

        @pl.when(cond)
        def _(other=other):
            pl.semaphore_signal(
                barrier, inc=1, device_id={"seq": other}, device_id_type=pl.DeviceIdType.MESH
            )

    pl.semaphore_wait(barrier, total)

    def at(i):
        return pl.ds(i * chunk, chunk)

    def copy(src, dst, si, ri, i, other):
        return pltpu.make_async_remote_copy(
            src_ref=src.at[at(i)],
            dst_ref=dst.at[at(i)],
            send_sem=send_sem.at[si, i],
            recv_sem=recv_sem.at[ri, i],
            device_id={"seq": other},
            device_id_type=pl.DeviceIdType.MESH,
        )

    away = lax.rem(c + 1, n)

    def arrived(ref, ri, i):
        copy(ref, ref, 0, ri, i, away).wait_recv()

    sends = [
        ("e", node, r_e, r_e, 1, 1, c + 1),
        ("e", inner, r_e, r_e, 2, 1, c + 4),
        ("f", (c != root) & (c < n - 1), s_f, r_f, 0, 0, c + 1),
        ("f", c == root, s_f, r_e, 1, 1, c + 1),
        ("f", c == root, s_f, r_e, 2, 1, prompt + 2),
        ("b", (c > 0) & (c != prompt), s_b, r_b, 3, 2, c - 1),
        ("x", node & (c - 4 >= prompt), s_x, r_x, 4, 3, c - 4),
        ("x", c == prompt, s_x, r_x, 4, 3, c - 1),
        ("x", c == prompt + 2, s_x, r_y, 4, 4, root),
    ]

    def dispatch(kind, i):
        for name, cond, src, dst, si, ri, other in sends:
            if name == kind:

                @pl.when(cond)
                def _(src=src, dst=dst, si=si, ri=ri, other=other):
                    copy(src, dst, si, ri, i, other).start()

    own = flags[0:1, :][None] > 0.5
    following = flags[1:2, :][None] > 0.5
    zeros = jnp.zeros((chunk,) + load.shape[1:], F32)
    e_depth = jnp.where(even, prompt + (c - prompt) // 4, prompt + (c - 1 - prompt) // 4 + 1)

    def inside(i):
        return (i >= 0) & (i < count)

    def fade(i):
        return jnp.concatenate(
            [decay[pl.ds(i * chunk + j, 1), :][None] for j in range(chunk)], axis=0
        )

    def step(t, carry):
        ie = t - e_depth

        @pl.when(branch & inside(ie))
        def _():
            arrived(r_e, 1, ie)
            dispatch("e", ie)

        i = t - c

        @pl.when(inside(i))
        def _():
            @pl.when((c > 0) & (c != prompt))
            def _():
                arrived(r_f, 0, i)

            @pl.when((c == 0) | (c == prompt))
            def _():
                r_f[at(i)] = zeros

            @pl.when(c < prompt)
            def _():
                r_e[at(i)] = zeros

            state = jnp.where(own, r_e[at(i)], r_f[at(i)])
            s_f[at(i)] = fade(i) * state + load[at(i)]
            dispatch("f", i)
            state_out[at(i)] = state.astype(BF16)

        k = t - (n - 1 - c)

        @pl.when(inside(k))
        def _():
            @pl.when((c < n - 1) & (c != root))
            def _():
                arrived(r_b, 2, k)

            @pl.when(c == n - 1)
            def _():
                r_b[at(k)] = zeros

            @pl.when(c == root)
            def _():
                arrived(r_x, 3, k)
                arrived(r_y, 4, k)
                r_b[at(k)] = r_x[at(k)] + r_y[at(k)]

            back = r_b[at(k)]
            held = jnp.where(following, 0.0, back)
            onward = fade(k) * held + gload[at(k)]
            s_b[at(k)] = onward
            dispatch("b", k)

            @pl.when(node)
            def _():
                @pl.when(inner)
                def _():
                    arrived(r_x, 3, k)

                @pl.when(jnp.logical_not(inner))
                def _():
                    r_x[at(k)] = zeros

                s_x[at(k)] = (
                    jnp.where(own, onward, 0.0) + jnp.where(following, back, 0.0) + r_x[at(k)]
                )
                dispatch("x", k)

            grad_out[at(k)] = held.astype(BF16)

        return carry

    lax.fori_loop(0, count + n - 1, step, 0)

    def drain(i, carry):
        for name, cond, src, dst, si, ri, other in sends:

            @pl.when(cond)
            def _(src=src, dst=dst, si=si, ri=ri, other=other):
                copy(src, dst, si, ri, i, other).wait_send()

        return carry

    lax.fori_loop(0, count, drain, 0)


def on_device(queries, keys, values, out_grad, decay_rate, block_parent, block_valid):
    rows, width = queries.shape
    heads = decay_rate.shape[0]
    size = width // heads
    n = lax.axis_size("seq")
    prompt = n // 4
    me = lax.axis_index("seq")
    places = jnp.arange(n)
    starts = (places >= prompt) & (block_parent == prompt - 1)
    following = (places == me + 1) & (me != prompt - 1)
    flags = jnp.stack(
        [jnp.any(starts & (places == me)), jnp.any(starts & following)]
    ).astype(F32)
    flags = jnp.broadcast_to(jnp.concatenate([flags, jnp.zeros((6,), F32)])[:, None], (8, size))
    valid = lax.dynamic_slice_in_dim(block_valid, me, 1)

    per = 2
    big = pltpu.CompilerParams(vmem_limit_bytes=48 * 2**20)
    smem = pl.BlockSpec(memory_space=pltpu.SMEM)
    wide = pl.BlockSpec((rows, per * size), lambda i: (0, i))
    mats = pl.BlockSpec((per, size, size), lambda i: (i, 0, 0))

    def whole(*shape):
        return pl.BlockSpec(shape, lambda i: (0,) * len(shape))

    states = jax.ShapeDtypeStruct((heads, size, size), F32)
    load, gload, cum, cum_t, decay = pl.pallas_call(
        functools.partial(local_kernel, per),
        grid=(heads // per,),
        in_specs=[smem, whole(heads, rows), wide, wide, wide, wide],
        out_specs=[mats, mats, whole(heads, rows), whole(rows, heads), whole(heads, size)],
        out_shape=[
            states,
            states,
            jax.ShapeDtypeStruct((heads, rows), F32),
            jax.ShapeDtypeStruct((rows, heads), F32),
            jax.ShapeDtypeStruct((heads, size), F32),
        ],
        compiler_params=big,
        name="local_states",
    )(valid, decay_rate, queries, keys, values, out_grad)

    chunk = 2
    count = heads // chunk
    vmem = pl.BlockSpec(memory_space=pltpu.VMEM)
    state_bf, grad_bf = pl.pallas_call(
        functools.partial(chain_kernel, n, prompt, chunk),
        in_specs=[vmem] * 4,
        out_specs=[vmem] * 2,
        out_shape=[jax.ShapeDtypeStruct((heads, size, size), BF16)] * 2,
        scratch_shapes=[pltpu.VMEM((heads, size, size), F32)] * 8
        + [pltpu.SemaphoreType.DMA((5, count)), pltpu.SemaphoreType.DMA((5, count))],
        compiler_params=pltpu.CompilerParams(
            collective_id=0, has_side_effects=True, vmem_limit_bytes=48 * 2**20
        ),
        name="tree_scan",
    )(load, gload, decay, flags)

    return pl.pallas_call(
        functools.partial(grads_kernel, per),
        grid=(heads // per,),
        in_specs=[smem, whole(heads, rows), whole(rows, heads), wide, wide, wide, wide, mats, mats],
        out_specs=[wide, wide, wide],
        out_shape=[jax.ShapeDtypeStruct((rows, width), BF16)] * 3,
        compiler_params=big,
        name="block_grads",
    )(valid, cum, cum_t, queries, keys, values, out_grad, state_bf, grad_bf)


def solution(mesh):
    rows = P(("groups", "seq"), None)
    placed = (rows, rows, rows, rows, P(None, ("groups", "seq")), P("groups"), P("groups"))
    return jax.shard_map(
        on_device, mesh=mesh, in_specs=placed, out_specs=(rows, rows, rows), check_vma=False
    )
```

time: 671 us -> 142 us (0.21)
  waiting for transfers between devices: 213 us -> 0 us
  local copies, waits for them, and re-layouts: 173 us -> 3.42 us
  Pallas kernels: 0 us -> 135 us
  other arithmetic: 137 us -> 2.67 us
  matrix products: 74.1 us -> 0 us
  blocking collectives: 36.8 us -> 0 us
  loops' own time: 19.1 us -> 0 us
  between operations: 14.5 us -> 0.67 us
    all_gather x2 -> x0, waiting for transfers between devices: 213 us -> none  [entering(): pieces = jax.tree.map(lambda part: lax.all_gather(part, axis), value)]
    pallas_call x0 -> x3, Pallas kernels: none -> 135 us  [the longest x1 92 us: on_device(): pl.pallas_call(functools.partial(chain_kernel, n, prompt, chunk), in_spec...]
    select_n x63 -> x0, other arithmetic: 114 us -> none  [the longest x60 98.7 us: hop(): jnp.where(position < mine, new, old)]
    dot_general x21 -> x0, matrix products: 74.1 us -> none  [the longest x4 18.7 us: inner_block(): jnp.einsum('hts,the->she', attn_mix, grad_grp, preferred_element_type=jnp...]
    dynamic_update_slice x20 -> x0, local copies, waits for them, and re-layouts: 53.3 us -> none  [the longest x8 28.3 us: inner_block(): lax.dynamic_update_slice_in_dim(value_sum, value_part, begin, 1)]
    dynamic_slice x52 -> x1, local copies, waits for them, and re-layouts: 44.2 us -> 1.23 us  [on_device(): valid = lax.dynamic_slice_in_dim(block_valid, me, 1)]
    unnamed x1 -> x0, blocking collectives: 36.8 us -> none
    rev x3 -> x0, local copies, waits for them, and re-layouts: 23.5 us -> none  [entering(): pieces = jax.tree.map(lambda part: part[::-1], pieces)]
  transfers between devices with their start and end apart: 3 -> 0, of which waited for: 2 -> 0; matrix products, arithmetic and copies ran while one was open for 32% -> 0% of each run, Pallas kernels for 0% -> 0%
where the time goes in v1:
time: 142 us; the launch traced here: 141 us
  Pallas kernels  135 us (95%)
  local copies, waits for them, and re-layouts  3.42 us (2%)
  other arithmetic  2.67 us (2%)
    pallas_call x1, Pallas kernels, on_device(): pl.pallas_call(functools.partial(chain_kernel, n, prompt, chunk), in_spec...  92 us
    pallas_call x1, Pallas kernels, on_device(): pl.pallas_call(functools.partial(grads_kernel, per), grid=(heads // per,)...  27.3 us
    pallas_call x1, Pallas kernels, on_device(): pl.pallas_call(functools.partial(local_kernel, per), grid=(heads // per,)...  15.4 us

profile of v1, /device:TPU:0, one launch (start us, length us, event | category | flops | bytes accessed | tf_op | source)
XLA Modules:
  0.0 141.4 jit_solution(13610717966103051052)
XLA Ops:
  0.6 1.2 dynamic_slice.3.valid
  1.9 1.3 and_reduce_fusion.1
  3.2 1.4 pad_add_fusion
  4.5 0.1 broadcast_in_dim.2.flags
  4.6 0.0 copy-start.2
  4.6 0.8 copy-done.2
  5.4 15.4 %local_states.1 = (f32[32,128,128]{2,1,0:T(8,128)S(1)}, f32[32,128,128]{2,1,0:T(8,128)S(1)}, f32[32,384]{1,0:T(8,128)S(1)}, f32[384,32]{1,0:T(8,128)S(1)}, f32[32,128]{1,0:T(8,128)S(1)}) custom-call(s32[1]{0:T(128)} %dynamic_slice.3.valid, f32[32,384]{1,0:T(8,128)S(1)} %copy-done.2, bf16[384,4096]{1,0:T(8,128)(2,1)} %q.3, bf16[384,4096]{1,0:T(8,128)(2,1)} %k.3, ...), custom_call_target="tpu_custom_call" | custom-call | tf_op jit(solution)/shard_map/local_states/pallas_call | solution.py:277
  20.8 0.0 copy-start.1
  20.8 1.3 copy-done.1
  22.1 0.0 copy-start
  22.1 92.0 %tree_scan.1 = (bf16[32,128,128]{2,1,0:T(8,128)(2,1)S(1)}, bf16[32,128,128]{2,1,0:T(8,128)(2,1)S(1)}) custom-call(f32[32,128,128]{2,1,0:T(8,128)S(1)} %get-tuple-element.12.load, f32[32,128,128]{2,1,0:T(8,128)} %copy-done.1, f32[32,128]{1,0:T(8,128)S(1)} %get-tuple-element.14.decay, f32[8,128]{1,0:T(8,128)S(1)} %broadcast_in_dim.2.flags), custom_call_target="tpu_custom_call" | custom-call | tf_op jit(solution)/shard_map/tree_scan/pallas_call | solution.py:296
  114.1 0.0 copy-done
  114.2 27.3 %block_grads.1 = (bf16[384,4096]{1,0:T(8,128)(2,1)}, bf16[384,4096]{1,0:T(8,128)(2,1)}, bf16[384,4096]{1,0:T(8,128)(2,1)}) custom-call(s32[1]{0:T(128)} %dynamic_slice.3.valid, f32[32,384]{1,0:T(8,128)S(1)} %get-tuple-element.10.cum, f32[384,32]{1,0:T(8,128)S(1)} %get-tuple-element.11.cum_t, bf16[384,4096]{1,0:T(8,128)(2,1)S(1)} %copy-done, ...), custom_call_target="tpu_custom_call" | custom-call | tf_op jit(solution)/shard_map/block_grads/pallas_call | solution.py:309
  (1 shorter events, 0.0 us)
Async XLA Ops:
  4.6 0.8 copy-start.2
  20.8 1.3 copy-start.1
  22.1 92.0 %copy-start = (bf16[384,4096]{1,0:T(8,128)(2,1)S(1)}, bf16[384,4096]{1,0:T(8,128)(2,1)}, u32[]{:S(2)}) copy-start(bf16[384,4096]{1,0:T(8,128)(2,1)} %q.3) | copy-start | bytes 9437188

commit v2 on v1

v2 whole, which is shorter than its diff:
```python
import functools

import jax
import jax.numpy as jnp
from jax import lax
from jax.experimental import pallas as pl
from jax.experimental.pallas import tpu as pltpu
from jax.sharding import PartitionSpec as P

F32 = jnp.float32
BF16 = jnp.bfloat16
TN = (((0,), (0,)), ((), ()))
NT = (((1,), (1,)), ((), ()))


def dot(a, b, dims=(((1,), (0,)), ((), ())), precision=None):
    return lax.dot_general(a, b, dims, precision=precision, preferred_element_type=F32)


def live_mask(valid, rows, width):
    return (lax.broadcasted_iota(jnp.int32, (rows, width), 0) < valid).astype(F32).astype(BF16)


def head_column(cum_t, head):
    lane = lax.broadcasted_iota(jnp.int32, cum_t.shape, 1)
    return jnp.sum(jnp.where(lane == head, cum_t, 0.0), axis=1, keepdims=True)


def scan_kernel(
    n, prompt, chunk, group, valid, rate, flags, q_hbm, k_hbm, v_hbm, g_hbm, dq_hbm, dk_hbm, dv_hbm,
    q, k, v, g, dq, dk, dv, cum, cum_t, decay, mask, load, gload, state_bf, grad_bf,
    r_f, r_e, r_b, r_x, r_y, s_x, in_sem, out_sem, send_sem, recv_sem,
):
    rows = q.shape[0]
    size = load.shape[1]
    span = group * size
    groups = load.shape[0] // group
    near = group // chunk
    fetches = ((q_hbm, q), (k_hbm, k), (v_hbm, v), (g_hbm, g))
    results = ((dq, dq_hbm), (dk, dk_hbm), (dv, dv_hbm))

    def columns(part):
        return pl.ds(pl.multiple_of(part * span, span), span)

    def fetch(which, part):
        src, dst = fetches[which]
        return pltpu.make_async_copy(
            src.at[:, columns(part)], dst.at[:, columns(part)], in_sem.at[which, part]
        )

    def store(which, part):
        src, dst = results[which]
        return pltpu.make_async_copy(
            src.at[:, columns(part)], dst.at[:, columns(part)], out_sem.at[which, part]
        )

    for part in range(groups):
        for which in range(4):
            fetch(which, part).start()

    c = lax.axis_index("seq")
    count = load.shape[0] // chunk
    root = prompt - 1
    branch = c >= prompt
    even = lax.rem(c, 2) == 0
    node = branch & even
    inner = node & (c + 4 < n)
    partners = [
        (c > 0, c - 1),
        (c < n - 1, c + 1),
        (inner, c + 4),
        (node & (c - 4 >= prompt), c - 4),
        (c == prompt + 2, root),
        (c == root, prompt + 2),
    ]
    barrier = pltpu.get_barrier_semaphore()
    total = 0
    for cond, other in partners:
        total = total + cond.astype(jnp.int32)

        @pl.when(cond)
        def _(other=other):
            pl.semaphore_signal(
                barrier, inc=1, device_id={"seq": other}, device_id_type=pl.DeviceIdType.MESH
            )

    pl.semaphore_wait(barrier, total)

    def at(i):
        return pl.ds(i * chunk, chunk)

    def copy(src, dst, si, ri, i, other):
        return pltpu.make_async_remote_copy(
            src_ref=src.at[at(i)],
            dst_ref=dst.at[at(i)],
            send_sem=send_sem.at[si, i],
            recv_sem=recv_sem.at[ri, i],
            device_id={"seq": other},
            device_id_type=pl.DeviceIdType.MESH,
        )

    away = lax.rem(c + 1, n)

    def arrived(ref, ri, i):
        copy(ref, ref, 0, ri, i, away).wait_recv()

    sends = [
        ("e", node, r_e, r_e, 1, 1, c + 1),
        ("e", inner, r_e, r_e, 2, 1, c + 4),
        ("f", (c != root) & (c < n - 1), load, r_f, 0, 0, c + 1),
        ("f", c == root, load, r_e, 1, 1, c + 1),
        ("f", c == root, load, r_e, 2, 1, prompt + 2),
        ("b", (c > 0) & (c != prompt), gload, r_b, 3, 2, c - 1),
        ("x", node & (c - 4 >= prompt), s_x, r_x, 4, 3, c - 4),
        ("x", c == prompt, s_x, r_x, 4, 3, c - 1),
        ("x", c == prompt + 2, s_x, r_y, 4, 4, root),
    ]

    def dispatch(kind, i):
        for name, cond, src, dst, si, ri, other in sends:
            if name == kind:

                @pl.when(cond)
                def _(src=src, dst=dst, si=si, ri=ri, other=other):
                    copy(src, dst, si, ri, i, other).start()


    place = lax.broadcasted_iota(jnp.int32, rate.shape, 1)
    log_decay = jnp.where(place < valid[0], -rate[...], 0.0)
    tri = (
        lax.broadcasted_iota(jnp.int32, (rows, rows), 0)
        >= lax.broadcasted_iota(jnp.int32, (rows, rows), 1)
    ).astype(F32)
    high = lax.Precision.HIGHEST
    cum[...] = dot(log_decay, tri, NT, high)
    cum_t[...] = dot(tri, log_decay, NT, high)
    decay[...] = jnp.broadcast_to(jnp.exp(cum[:, rows - 1 : rows]), decay.shape)
    mask[...] = live_mask(valid[0], rows, size)

    def head_columns(head):
        return pl.ds(pl.multiple_of(head * size, size), size)

    def local_states(i):
        for part in range(chunk):
            head = i * chunk + part
            cols = head_columns(head)
            column = head_column(cum_t[...], head)
            head_w = jnp.exp(column)
            tail_w = jnp.exp(column[rows - 1 :, :] - column)
            live = mask[...]
            qm, km, vm, gm = (ref[:, cols] * live for ref in (q, k, v, g))
            q[:, cols] = qm
            k[:, cols] = km
            v[:, cols] = vm
            g[:, cols] = gm
            load[head] = dot((tail_w * km.astype(F32)).astype(BF16), vm, TN)
            gload[head] = dot((head_w * qm.astype(F32)).astype(BF16), gm, TN)

    def block_grads(i):
        for part in range(chunk):
            head = i * chunk + part
            cols = head_columns(head)
            column = head_column(cum_t[...], head)
            row = cum[pl.ds(head, 1), :]
            head_w = jnp.exp(column)
            tail_w = jnp.exp(column[rows - 1 :, :] - column)
            causal_t = lax.broadcasted_iota(jnp.int32, (rows, rows), 0) <= (
                lax.broadcasted_iota(jnp.int32, (rows, rows), 1)
            )
            qm, km, vm, gm = (ref[:, cols] for ref in (q, k, v, g))
            weight_t = jnp.where(causal_t, jnp.exp(jnp.minimum(row - column, 0.0)), 0.0)
            attn_t = (dot(km, qm, NT) * weight_t).astype(BF16)
            gmix_t = (dot(vm, gm, NT) * weight_t).astype(BF16)
            state = state_bf[head]
            grad = grad_bf[head]
            dq[:, cols] = (dot(gmix_t, km, TN) + head_w * dot(gm, state, NT)).astype(BF16)
            dk[:, cols] = (dot(gmix_t, qm) + tail_w * dot(vm, grad, NT)).astype(BF16)
            dv[:, cols] = (dot(attn_t, gm) + tail_w * dot(km, grad)).astype(BF16)

    own = flags[0:1, :][None] > 0.5
    following = flags[1:2, :][None] > 0.5
    zeros = jnp.zeros((chunk,) + load.shape[1:], F32)
    e_depth = jnp.where(even, prompt + (c - prompt) // 4, prompt + (c - 1 - prompt) // 4 + 1)

    def inside(i):
        return (i >= 0) & (i < count)

    def fade(i):
        return jnp.concatenate(
            [decay[pl.ds(i * chunk + j, 1), :][None] for j in range(chunk)], axis=0
        )

    def step(t, carry):
        ie = t - e_depth

        @pl.when(branch & inside(ie))
        def _():
            arrived(r_e, 1, ie)
            dispatch("e", ie)

        i = t - c

        @pl.when(inside(i))
        def _():
            @pl.when((c > 0) & (c != prompt))
            def _():
                arrived(r_f, 0, i)

            @pl.when((c == 0) | (c == prompt))
            def _():
                r_f[at(i)] = zeros

            @pl.when(c < prompt)
            def _():
                r_e[at(i)] = zeros

            state = jnp.where(own, r_e[at(i)], r_f[at(i)])
            load[at(i)] = fade(i) * state + load[at(i)]
            dispatch("f", i)
            state_bf[at(i)] = state.astype(BF16)

        j = t - (n - 1 - c)

        @pl.when(inside(j))
        def _():
            @pl.when((c < n - 1) & (c != root))
            def _():
                arrived(r_b, 2, j)

            @pl.when(c == n - 1)
            def _():
                r_b[at(j)] = zeros

            @pl.when(c == root)
            def _():
                arrived(r_x, 3, j)
                arrived(r_y, 4, j)
                r_b[at(j)] = r_x[at(j)] + r_y[at(j)]

            back = r_b[at(j)]
            held = jnp.where(following, 0.0, back)
            onward = fade(j) * held + gload[at(j)]
            gload[at(j)] = onward
            dispatch("b", j)

            @pl.when(node)
            def _():
                @pl.when(inner)
                def _():
                    arrived(r_x, 3, j)

                @pl.when(jnp.logical_not(inner))
                def _():
                    r_x[at(j)] = zeros

                s_x[at(j)] = (
                    jnp.where(own, onward, 0.0) + jnp.where(following, back, 0.0) + r_x[at(j)]
                )
                dispatch("x", j)

            grad_bf[at(j)] = held.astype(BF16)

        last = t - jnp.maximum(c, n - 1 - c)

        @pl.when(inside(last))
        def _():
            block_grads(last)

            @pl.when(lax.rem(last, near) == near - 1)
            def _():
                for which in range(3):
                    store(which, last // near).start()

        first = t + 1 - jnp.minimum(c, n - 1 - c)

        @pl.when(inside(first))
        def _():
            @pl.when(lax.rem(first, near) == 0)
            def _():
                for which in range(4):
                    fetch(which, first // near).wait()

            local_states(first)

        return carry

    lax.fori_loop(-1, count + n - 1, step, 0)

    def drain(i, carry):
        for name, cond, src, dst, si, ri, other in sends:

            @pl.when(cond)
            def _(src=src, dst=dst, si=si, ri=ri, other=other):
                copy(src, dst, si, ri, i, other).wait_send()

        return carry

    lax.fori_loop(0, count, drain, 0)

    for part in range(groups):
        for which in range(3):
            store(which, part).wait()


def on_device(queries, keys, values, out_grad, decay_rate, block_parent, block_valid):
    rows, width = queries.shape
    heads = decay_rate.shape[0]
    size = width // heads
    n = lax.axis_size("seq")
    prompt = n // 4
    me = lax.axis_index("seq")
    places = jnp.arange(n)
    starts = (places >= prompt) & (block_parent == prompt - 1)
    following = (places == me + 1) & (me != prompt - 1)
    flags = jnp.stack(
        [jnp.any(starts & (places == me)), jnp.any(starts & following)]
    ).astype(F32)
    flags = jnp.broadcast_to(jnp.concatenate([flags, jnp.zeros((6,), F32)])[:, None], (8, size))
    valid = lax.dynamic_slice_in_dim(block_valid, me, 1)

    chunk = 2
    group = 8
    count = heads // chunk
    vmem = pl.BlockSpec(memory_space=pltpu.VMEM)
    hbm = pl.BlockSpec(memory_space=pl.ANY)
    tall = pltpu.VMEM((rows, width), BF16)
    states = pltpu.VMEM((heads, size, size), F32)
    states_bf = pltpu.VMEM((heads, size, size), BF16)
    return pl.pallas_call(
        functools.partial(scan_kernel, n, prompt, chunk, group),
        in_specs=[pl.BlockSpec(memory_space=pltpu.SMEM), vmem, vmem] + [hbm] * 4,
        out_specs=[hbm] * 3,
        out_shape=[jax.ShapeDtypeStruct((rows, width), BF16)] * 3,
        scratch_shapes=[tall] * 7
        + [
            pltpu.VMEM((heads, rows), F32),
            pltpu.VMEM((rows, heads), F32),
            pltpu.VMEM((heads, size), F32),
            pltpu.VMEM((rows, size), BF16),
        ]
        + [states] * 2
        + [states_bf] * 2
        + [states] * 6
        + [
            pltpu.SemaphoreType.DMA((4, heads // group)),
            pltpu.SemaphoreType.DMA((3, heads // group)),
            pltpu.SemaphoreType.DMA((5, count)),
            pltpu.SemaphoreType.DMA((5, count)),
        ],
        compiler_params=pltpu.CompilerParams(
            collective_id=0, has_side_effects=True, vmem_limit_bytes=56 * 2**20
        ),
        name="tree_scan",
    )(valid, decay_rate, flags, queries, keys, values, out_grad)


def solution(mesh):
    rows = P(("groups", "seq"), None)
    placed = (rows, rows, rows, rows, P(None, ("groups", "seq")), P("groups"), P("groups"))
    return jax.shard_map(
        on_device, mesh=mesh, in_specs=placed, out_specs=(rows, rows, rows), check_vma=False
    )
```

time: 142 us -> 116 us (0.82)
  Pallas kernels: 135 us -> 102 us
  local copies, waits for them, and re-layouts: 3.42 us -> 10.7 us
    pallas_call x3 -> x1, Pallas kernels: 135 us -> 102 us  [on_device(): pl.pallas_call(functools.partial(scan_kernel, n, prompt, chunk, group), i...]
    unnamed x6 -> x7, local copies, waits for them, and re-layouts: 2.12 us -> 8.75 us
where the time goes in v2:
time: 116 us
  Pallas kernels  102 us (88%)
  local copies, waits for them, and re-layouts  10.7 us (9%)
  other arithmetic  2.67 us (2%)
    pallas_call x1, Pallas kernels, on_device(): pl.pallas_call(functools.partial(scan_kernel, n, prompt, chunk, group), i...  102 us
    unnamed x7, local copies, waits for them, and re-layouts  8.75 us

profile of v2, /device:TPU:0, one launch (start us, length us, event | category | flops | bytes accessed | tf_op | source)
XLA Modules:
  0.0 116.2 jit_solution(17852829310616567262)
XLA Ops:
  0.6 1.2 %dynamic_slice.3.valid = s32[1]{0:T(128)} dynamic-slice(s32[16]{0:T(128)} %param.13, s32[]{:T(128)S(6)} %select_n.3), dynamic_slice_sizes={1} | dynamic-slice | bytes 12 | tf_op jit(solution)/shard_map/dynamic_slice | solution.py:319
  1.9 1.3 %and_reduce_fusion.1 = (pred[]{:T(512)}, pred[]{:T(512)}) fusion(s32[]{:T(128)S(6)} %axis_index.12, s32[16]{0:T(128)} %param.12, pred[]{:T(512)S(6)} %ne.3, s32[]{:T(128)S(6)} %add.7), kind=kLoop, calls=%fused_computation.3 | loop fusion | flops 158 | bytes 75 | tf_op jit(solution)/shard_map/reduce_or | solution.py:316
  3.2 1.4 %pad_add_fusion = pred[2]{0:T(512)(128)(4,1)S(1)} fusion(pred[1]{0:T(512)(128)(4,1)} %bitcast.1, pred[1]{0:T(512)(128)(4,1)} %bitcast), kind=kLoop, calls=%fused_computation | loop fusion | flops 2 | bytes 4 | tf_op jit(solution)/shard_map/stack | solution.py:315
  4.6 0.7 broadcast_in_dim.2.flags
  5.2 102.2 %tree_scan.1 = (bf16[384,4096]{1,0:T(8,128)(2,1)}, bf16[384,4096]{1,0:T(8,128)(2,1)}, bf16[384,4096]{1,0:T(8,128)(2,1)}) custom-call(s32[1]{0:T(128)} %dynamic_slice.3.valid, f32[32,384]{1,0:T(8,128)} %rate.1, f32[8,128]{1,0:T(8,128)} %broadcast_in_dim.2.flags, bf16[384,4096]{1,0:T(8,128)(2,1)} %q_hbm.1, bf16[384,4096]{1,0:T(8,128)(2,1)} %k_hbm.1, ...), custom_call_target="tpu_custom_call" | custom-call | tf_op jit(solution)/shard_map/tree_scan/pallas_call | solution.py:329
  107.4 0.0 copy-start.1
  107.4 4.1 %copy.13 = bf16[384,4096]{1,0:T(8,128)(2,1)} copy(bf16[384,4096]{1,0:T(8,128)(2,1)} %get-tuple-element.8) | data formatting | bytes 6291456
  111.5 0.0 copy-done.1
  111.5 0.0 copy-start
  111.5 1.7 %copy.14 = bf16[384,4096]{1,0:T(8,128)(2,1)} copy(bf16[384,4096]{1,0:T(8,128)(2,1)S(1)} %copy-done.1) | data formatting | bytes 6291456
  113.2 1.4 %copy-done = bf16[384,4096]{1,0:T(8,128)(2,1)S(1)} copy-done((bf16[384,4096]{1,0:T(8,128)(2,1)S(1)}, bf16[384,4096]{1,0:T(8,128)(2,1)}, u32[]{:S(2)}) %copy-start) | copy-done | bytes 3145752
  114.5 1.7 %copy.15 = bf16[384,4096]{1,0:T(8,128)(2,1)} copy(bf16[384,4096]{1,0:T(8,128)(2,1)S(1)} %copy-done) | data formatting | bytes 6291456
  (1 shorter events, 0.0 us)
Async XLA Ops:
  107.4 4.1 %copy-start.1 = (bf16[384,4096]{1,0:T(8,128)(2,1)S(1)}, bf16[384,4096]{1,0:T(8,128)(2,1)}, u32[]{:S(2)}) copy-start(bf16[384,4096]{1,0:T(8,128)(2,1)} %get-tuple-element.9) | copy-start | bytes 9437188
  111.5 3.0 %copy-start = (bf16[384,4096]{1,0:T(8,128)(2,1)S(1)}, bf16[384,4096]{1,0:T(8,128)(2,1)}, u32[]{:S(2)}) copy-start(bf16[384,4096]{1,0:T(8,128)(2,1)} %get-tuple-element.10) | copy-start | bytes 9437188

commit v3 on v2

--- a/solution.py
+++ b/solution.py
@@ -27,7 +27,7 @@
 
 
 def scan_kernel(
-    n, prompt, chunk, group, valid, rate, flags, q_hbm, k_hbm, v_hbm, g_hbm, dq_hbm, dk_hbm, dv_hbm,
+    n, prompt, chunk, group, lag, cut, parent, valid_rows, rate, q_hbm, k_hbm, v_hbm, g_hbm, dq_hbm, dk_hbm, dv_hbm,
     q, k, v, g, dq, dk, dv, cum, cum_t, decay, mask, load, gload, state_bf, grad_bf,
     r_f, r_e, r_b, r_x, r_y, s_x, in_sem, out_sem, send_sem, recv_sem,
 ):
@@ -125,8 +125,9 @@
                     copy(src, dst, si, ri, i, other).start()
 
 
+    valid = valid_rows[c]
     place = lax.broadcasted_iota(jnp.int32, rate.shape, 1)
-    log_decay = jnp.where(place < valid[0], -rate[...], 0.0)
+    log_decay = jnp.where(place < valid, -rate[...], 0.0)
     tri = (
         lax.broadcasted_iota(jnp.int32, (rows, rows), 0)
         >= lax.broadcasted_iota(jnp.int32, (rows, rows), 1)
@@ -135,7 +136,7 @@
     cum[...] = dot(log_decay, tri, NT, high)
     cum_t[...] = dot(tri, log_decay, NT, high)
     decay[...] = jnp.broadcast_to(jnp.exp(cum[:, rows - 1 : rows]), decay.shape)
-    mask[...] = live_mask(valid[0], rows, size)
+    mask[...] = live_mask(valid, rows, size)
 
     def head_columns(head):
         return pl.ds(pl.multiple_of(head * size, size), size)
@@ -164,21 +165,41 @@
             row = cum[pl.ds(head, 1), :]
             head_w = jnp.exp(column)
             tail_w = jnp.exp(column[rows - 1 :, :] - column)
-            causal_t = lax.broadcasted_iota(jnp.int32, (rows, rows), 0) <= (
-                lax.broadcasted_iota(jnp.int32, (rows, rows), 1)
+            qm, km, vm, gm = (ref[:, cols] for ref in (q, k, v, g))
+            inner_q = [None] * (rows // cut)
+            inner_k, inner_v = [], []
+            for low in range(0, rows, cut):
+                here = slice(low, low + cut)
+                weight_t = jnp.exp(jnp.minimum(row[:, low:] - column[here], 0.0))
+                causal_t = lax.broadcasted_iota(jnp.int32, weight_t.shape, 0) <= (
+                    lax.broadcasted_iota(jnp.int32, weight_t.shape, 1)
+                )
+                weight_t = jnp.where(causal_t, weight_t, 0.0)
+                attn_t = (dot(km[here], qm[low:], NT) * weight_t).astype(BF16)
+                gmix_t = (dot(vm[here], gm[low:], NT) * weight_t).astype(BF16)
+                query_part = dot(gmix_t, km[here], TN)
+                for later in range(low, rows, cut):
+                    piece = query_part[later - low : later - low + cut]
+                    held = inner_q[later // cut]
+                    inner_q[later // cut] = piece if held is None else held + piece
+                inner_k.append(dot(gmix_t, qm[low:]))
+                inner_v.append(dot(attn_t, gm[low:]))
+            query_in, key_in, value_in = (
+                jnp.concatenate(parts, axis=0) for parts in (inner_q, inner_k, inner_v)
             )
-            qm, km, vm, gm = (ref[:, cols] for ref in (q, k, v, g))
-            weight_t = jnp.where(causal_t, jnp.exp(jnp.minimum(row - column, 0.0)), 0.0)
-            attn_t = (dot(km, qm, NT) * weight_t).astype(BF16)
-            gmix_t = (dot(vm, gm, NT) * weight_t).astype(BF16)
             state = state_bf[head]
             grad = grad_bf[head]
-            dq[:, cols] = (dot(gmix_t, km, TN) + head_w * dot(gm, state, NT)).astype(BF16)
-            dk[:, cols] = (dot(gmix_t, qm) + tail_w * dot(vm, grad, NT)).astype(BF16)
-            dv[:, cols] = (dot(attn_t, gm) + tail_w * dot(km, grad)).astype(BF16)
-
-    own = flags[0:1, :][None] > 0.5
-    following = flags[1:2, :][None] > 0.5
+            dq[:, cols] = (query_in + head_w * dot(gm, state, NT)).astype(BF16)
+            dk[:, cols] = (key_in + tail_w * dot(vm, grad, NT)).astype(BF16)
+            dv[:, cols] = (value_in + tail_w * dot(km, grad)).astype(BF16)
+
+    def starts(block):
+        held = parent[jnp.minimum(block, n - 1)]
+        here = jnp.where((block >= prompt) & (block < n) & (c != root), root, -2)
+        return jnp.full((1, 1, size), held, jnp.int32) == here
+
+    own = starts(c)
+    following = starts(c + 1)
     zeros = jnp.zeros((chunk,) + load.shape[1:], F32)
     e_depth = jnp.where(even, prompt + (c - prompt) // 4, prompt + (c - 1 - prompt) // 4 + 1)
 
@@ -191,14 +212,14 @@
         )
 
     def step(t, carry):
-        ie = t - e_depth
+        ie = t - lag * e_depth
 
         @pl.when(branch & inside(ie))
         def _():
             arrived(r_e, 1, ie)
             dispatch("e", ie)
 
-        i = t - c
+        i = t - lag * c
 
         @pl.when(inside(i))
         def _():
@@ -219,7 +240,7 @@
             dispatch("f", i)
             state_bf[at(i)] = state.astype(BF16)
 
-        j = t - (n - 1 - c)
+        j = t - lag * (n - 1 - c)
 
         @pl.when(inside(j))
         def _():
@@ -260,7 +281,7 @@
 
             grad_bf[at(j)] = held.astype(BF16)
 
-        last = t - jnp.maximum(c, n - 1 - c)
+        last = t - lag * jnp.maximum(c, n - 1 - c)
 
         @pl.when(inside(last))
         def _():
@@ -271,7 +292,7 @@
                 for which in range(3):
                     store(which, last // near).start()
 
-        first = t + 1 - jnp.minimum(c, n - 1 - c)
+        first = t + 1
 
         @pl.when(inside(first))
         def _():
@@ -284,7 +305,7 @@
 
         return carry
 
-    lax.fori_loop(-1, count + n - 1, step, 0)
+    lax.fori_loop(-1, count + lag * (n - 1), step, 0)
 
     def drain(i, carry):
         for name, cond, src, dst, si, ri, other in sends:
@@ -308,27 +329,20 @@
     size = width // heads
     n = lax.axis_size("seq")
     prompt = n // 4
-    me = lax.axis_index("seq")
-    places = jnp.arange(n)
-    starts = (places >= prompt) & (block_parent == prompt - 1)
-    following = (places == me + 1) & (me != prompt - 1)
-    flags = jnp.stack(
-        [jnp.any(starts & (places == me)), jnp.any(starts & following)]
-    ).astype(F32)
-    flags = jnp.broadcast_to(jnp.concatenate([flags, jnp.zeros((6,), F32)])[:, None], (8, size))
-    valid = lax.dynamic_slice_in_dim(block_valid, me, 1)
-
-    chunk = 2
+    chunk = 1
     group = 8
+    lag = 3
+    cut = rows
     count = heads // chunk
+    smem = pl.BlockSpec(memory_space=pltpu.SMEM)
     vmem = pl.BlockSpec(memory_space=pltpu.VMEM)
     hbm = pl.BlockSpec(memory_space=pl.ANY)
     tall = pltpu.VMEM((rows, width), BF16)
     states = pltpu.VMEM((heads, size, size), F32)
     states_bf = pltpu.VMEM((heads, size, size), BF16)
     return pl.pallas_call(
-        functools.partial(scan_kernel, n, prompt, chunk, group),
-        in_specs=[pl.BlockSpec(memory_space=pltpu.SMEM), vmem, vmem] + [hbm] * 4,
+        functools.partial(scan_kernel, n, prompt, chunk, group, lag, cut),
+        in_specs=[smem, smem, vmem] + [hbm] * 4,
         out_specs=[hbm] * 3,
         out_shape=[jax.ShapeDtypeStruct((rows, width), BF16)] * 3,
         scratch_shapes=[tall] * 7
@@ -351,7 +365,7 @@
             collective_id=0, has_side_effects=True, vmem_limit_bytes=56 * 2**20
         ),
         name="tree_scan",
-    )(valid, decay_rate, flags, queries, keys, values, out_grad)
+    )(block_parent, block_valid, decay_rate, queries, keys, values, out_grad)
 
 
 def solution(mesh):

time: 116 us -> 100 us (0.86)
  Pallas kernels: 102 us -> 90.7 us
  other arithmetic: 2.67 us -> 0 us
  local copies, waits for them, and re-layouts: 10.7 us -> 8.75 us
    pallas_call x1, Pallas kernels: 102 us -> 90.7 us  [on_device(): pl.pallas_call(functools.partial(scan_kernel, n, prompt, chunk, group, la...]
    another operation x1 -> x0, other arithmetic: 1.37 us -> none  [on_device(): jnp.stack([jnp.any(starts & (places == me)), jnp.any(starts & following)])]
    reduce_or x1 -> x0, other arithmetic: 1.3 us -> none  [on_device(): jnp.any(starts & (places == me))]
    dynamic_slice x1 -> x0, local copies, waits for them, and re-layouts: 1.24 us -> none  [on_device(): valid = lax.dynamic_slice_in_dim(block_valid, me, 1)]
where the time goes in v3:
time: 100 us
  Pallas kernels  90.7 us (91%)
  local copies, waits for them, and re-layouts  8.75 us (9%)
    pallas_call x1, Pallas kernels, on_device(): pl.pallas_call(functools.partial(scan_kernel, n, prompt, chunk, group, la...  90.7 us
    unnamed x7, local copies, waits for them, and re-layouts  8.75 us

profile of v3, /device:TPU:0, one launch (start us, length us, event | category | flops | bytes accessed | tf_op | source)
XLA Modules:
  0.0 100.1 jit_solution(14709290957102250626)
XLA Ops:
  0.6 90.7 %tree_scan.1 = (bf16[384,4096]{1,0:T(8,128)(2,1)}, bf16[384,4096]{1,0:T(8,128)(2,1)}, bf16[384,4096]{1,0:T(8,128)(2,1)}) custom-call(s32[16]{0:T(128)} %parent.1, s32[16]{0:T(128)} %valid_rows.1, f32[32,384]{1,0:T(8,128)} %rate.1, bf16[384,4096]{1,0:T(8,128)(2,1)} %q_hbm.1, bf16[384,4096]{1,0:T(8,128)(2,1)} %k_hbm.1, bf16[384,4096]{1,0:T(8,128)(2,1)} %v_hbm.1, ...), custom_call_target="tpu_custom_call" | custom-call | tf_op jit(solution)/shard_map/tree_scan/pallas_call | solution.py:343
  91.4 0.0 copy-start.1
  91.4 4.1 %copy.13 = bf16[384,4096]{1,0:T(8,128)(2,1)} copy(bf16[384,4096]{1,0:T(8,128)(2,1)} %get-tuple-element.6) | data formatting | bytes 6291456
  95.4 0.0 copy-done.1
  95.4 0.0 copy-start
  95.4 1.7 %copy.14 = bf16[384,4096]{1,0:T(8,128)(2,1)} copy(bf16[384,4096]{1,0:T(8,128)(2,1)S(1)} %copy-done.1) | data formatting | bytes 6291456
  97.1 1.4 %copy-done = bf16[384,4096]{1,0:T(8,128)(2,1)S(1)} copy-done((bf16[384,4096]{1,0:T(8,128)(2,1)S(1)}, bf16[384,4096]{1,0:T(8,128)(2,1)}, u32[]{:S(2)}) %copy-start) | copy-done | bytes 3145752
  98.5 1.7 %copy.15 = bf16[384,4096]{1,0:T(8,128)(2,1)} copy(bf16[384,4096]{1,0:T(8,128)(2,1)S(1)} %copy-done) | data formatting | bytes 6291456
Async XLA Ops:
  91.4 4.1 %copy-start.1 = (bf16[384,4096]{1,0:T(8,128)(2,1)S(1)}, bf16[384,4096]{1,0:T(8,128)(2,1)}, u32[]{:S(2)}) copy-start(bf16[384,4096]{1,0:T(8,128)(2,1)} %get-tuple-element.7) | copy-start | bytes 9437188
  95.4 3.0 %copy-start = (bf16[384,4096]{1,0:T(8,128)(2,1)S(1)}, bf16[384,4096]{1,0:T(8,128)(2,1)}, u32[]{:S(2)}) copy-start(bf16[384,4096]{1,0:T(8,128)(2,1)} %get-tuple-element.8) | copy-start | bytes 9437188

commit v4 on v3

--- a/solution.py
+++ b/solution.py
@@ -281,7 +281,7 @@
 
             grad_bf[at(j)] = held.astype(BF16)
 
-        last = t - lag * jnp.maximum(c, n - 1 - c)
+        last = t - lag * (n - 1)
 
         @pl.when(inside(last))
         def _():
@@ -331,7 +331,7 @@
     prompt = n // 4
     chunk = 1
     group = 8
-    lag = 3
+    lag = 2
     cut = rows
     count = heads // chunk
     smem = pl.BlockSpec(memory_space=pltpu.SMEM)

time: 100 us -> 101 us (1.010)
  no operation moved by 1% of the time
where the time goes in v4:
time: 101 us
  Pallas kernels  91.4 us (90%)
  local copies, waits for them, and re-layouts  8.75 us (9%)
    pallas_call x1, Pallas kernels, on_device(): pl.pallas_call(functools.partial(scan_kernel, n, prompt, chunk, group, la...  91.4 us
    unnamed x7, local copies, waits for them, and re-layouts  8.75 us

profile of v4, /device:TPU:0, one launch (start us, length us, event | category | flops | bytes accessed | tf_op | source)
XLA Modules:
  0.0 100.8 jit_solution(7311682928218533996)
XLA Ops:
  0.6 91.4 %tree_scan.1 = (bf16[384,4096]{1,0:T(8,128)(2,1)}, bf16[384,4096]{1,0:T(8,128)(2,1)}, bf16[384,4096]{1,0:T(8,128)(2,1)}) custom-call(s32[16]{0:T(128)} %parent.1, s32[16]{0:T(128)} %valid_rows.1, f32[32,384]{1,0:T(8,128)} %rate.1, bf16[384,4096]{1,0:T(8,128)(2,1)} %q_hbm.1, bf16[384,4096]{1,0:T(8,128)(2,1)} %k_hbm.1, bf16[384,4096]{1,0:T(8,128)(2,1)} %v_hbm.1, ...), custom_call_target="tpu_custom_call" | custom-call | tf_op jit(solution)/shard_map/tree_scan/pallas_call | solution.py:343
  92.0 0.0 copy-start.1
  92.0 4.1 %copy.13 = bf16[384,4096]{1,0:T(8,128)(2,1)} copy(bf16[384,4096]{1,0:T(8,128)(2,1)} %get-tuple-element.6) | data formatting | bytes 6291456
  96.1 0.0 copy-done.1
  96.1 0.0 copy-start
  96.1 1.7 %copy.14 = bf16[384,4096]{1,0:T(8,128)(2,1)} copy(bf16[384,4096]{1,0:T(8,128)(2,1)S(1)} %copy-done.1) | data formatting | bytes 6291456
  97.8 1.4 %copy-done = bf16[384,4096]{1,0:T(8,128)(2,1)S(1)} copy-done((bf16[384,4096]{1,0:T(8,128)(2,1)S(1)}, bf16[384,4096]{1,0:T(8,128)(2,1)}, u32[]{:S(2)}) %copy-start) | copy-done | bytes 3145752
  99.1 1.7 %copy.15 = bf16[384,4096]{1,0:T(8,128)(2,1)} copy(bf16[384,4096]{1,0:T(8,128)(2,1)S(1)} %copy-done) | data formatting | bytes 6291456
Async XLA Ops:
  92.0 4.1 %copy-start.1 = (bf16[384,4096]{1,0:T(8,128)(2,1)S(1)}, bf16[384,4096]{1,0:T(8,128)(2,1)}, u32[]{:S(2)}) copy-start(bf16[384,4096]{1,0:T(8,128)(2,1)} %get-tuple-element.7) | copy-start | bytes 9437188
  96.1 3.0 %copy-start = (bf16[384,4096]{1,0:T(8,128)(2,1)S(1)}, bf16[384,4096]{1,0:T(8,128)(2,1)}, u32[]{:S(2)}) copy-start(bf16[384,4096]{1,0:T(8,128)(2,1)} %get-tuple-element.8) | copy-start | bytes 9437188
